TPU v7x, 256 devices: a whole 4x4x8 slice. The times are simulated.
256 devices in a mesh: tm: 32 (over z, x), tmpl: 8 (over y, core).
Axes of the slice: x: 4, y: 4, z: 8, core: 2. Of those that a mesh axis runs over, the one named last changes fastest.
Arguments:
- strain: float32 [2, 3, 4194304], P(None, None, 'tm'), may hold values from -6 to 6
- templates: float32 [2, 8, 2048, 2048], P(None, 'tmpl', 'tm'), may hold values from -6 to 6
- pattern: int32 [8, 1024], P('tmpl'), may hold values 0 or 1
- cutoff: int32 [8], P('tmpl'), may hold values from 256 to 1024
Outputs:
- snr_power: float32 [8, 4194304], P('tmpl', 'tm')
- bank_peak: float32 [4194304], P('tm')
All inputs are finite; a program needn't handle non-finite values. No bound on the sum of `pattern` on one device may be relied on, other than what follows from the above.
Results may differ from a plain program's by a relative error of at most 0.000092.
Values sent between devices are 32-bit elements; how exact they have to be, the bound alone decides.
No kernel may reach another device: no remote copies, remote signals or barrier semaphores. Data moves between devices by JAX's collectives and lax.ppermute only.
A program may use at most 128 MiB of HBM per device.

v0:
```python
import math

import jax
import jax.numpy as jnp
from jax import lax
from jax.sharding import PartitionSpec as P

INNER = 32


EPSILON = 1e-06
HIGHEST = lax.Precision.HIGHEST


def phase_table(row_index, col_index, period, orient):
    product = row_index[:, None] * col_index[None, :] % period
    angle = orient * 2.0 * math.pi / period * product.astype(jnp.float32)
    return (jnp.cos(angle), jnp.sin(angle))


def rotate(stacked, cosine, sine_part):
    real_part = stacked[0] * cosine - stacked[1] * sine_part
    imag_part = stacked[0] * sine_part + stacked[1] * cosine
    return jnp.stack((real_part, imag_part))


def complex_table(real_part, imag_part):
    return jnp.stack((jnp.stack((real_part, imag_part)), jnp.stack((-imag_part, real_part))))


def dft_last(stacked, orient, first_factor):
    length_all = stacked.shape[-1]
    second_factor = length_all // first_factor
    leading = stacked.shape[1:-1]
    middle = stacked.size // (2 * length_all)
    folded = stacked.reshape(2, middle, first_factor, second_factor)
    first_idx = jnp.arange(first_factor, dtype=jnp.int32)
    second_idx = jnp.arange(second_factor, dtype=jnp.int32)
    cos_first, sin_first = phase_table(first_idx, first_idx, first_factor, orient)
    table_one = complex_table(cos_first, sin_first)
    section_one = jnp.einsum("pmab,pqak->qmkb", folded, table_one, precision=HIGHEST)
    cos_twist, sin_twist = phase_table(first_idx, second_idx, length_all, orient)
    cos_second, sin_second = phase_table(second_idx, second_idx, second_factor, orient)
    joint_real = cos_twist[:, :, None] * cos_second[None] - sin_twist[:, :, None] * sin_second[None]
    joint_imag = cos_twist[:, :, None] * sin_second[None] + sin_twist[:, :, None] * cos_second[None]
    table_two = complex_table(joint_real, joint_imag)
    section_two = jnp.einsum("qmkb,qrkbj->rmjk", section_one, table_two, precision=HIGHEST)
    return section_two.reshape((2,) + leading + (length_all,))


def local(strain, templates, pattern, cutoff):
    lane_index = lax.axis_index("tm")
    side_length = templates.shape[-1]
    local_side = templates.shape[2]
    full_length = side_length * side_length
    detectors = strain.shape[1]
    every_side = jnp.arange(side_length, dtype=jnp.int32)
    segment = strain.reshape(2, detectors, local_side, side_length)
    columns_a = lax.all_to_all(segment, "tm", split_axis=3, concat_axis=2, tiled=True)
    first_pass = dft_last(jnp.swapaxes(columns_a, 2, 3), -1.0, INNER)
    column_index = lane_index * local_side + jnp.arange(local_side, dtype=jnp.int32)
    cos_glob, sin_glob = phase_table(column_index, every_side, full_length, -1.0)
    first_pass = rotate(first_pass, cos_glob, sin_glob)
    bins_rows = lax.all_to_all(first_pass, "tm", split_axis=3, concat_axis=2, tiled=True)
    spectrum = dft_last(jnp.swapaxes(bins_rows, 2, 3), -1.0, INNER)
    block_index = jnp.arange(pattern.shape[1], dtype=jnp.int32)
    active = pattern.astype(jnp.float32) * (block_index[None, :] < cutoff[:, None]).astype(
        jnp.float32
    )
    weight = jnp.repeat(active, side_length // pattern.shape[1], axis=1)
    masked = templates * weight[None, :, None, :]
    local_norm = jnp.sum(masked[0] * masked[0] + masked[1] * masked[1], axis=(1, 2))
    norm_sq = lax.psum(local_norm, "tm")
    scaling = 1.0 / jnp.sqrt(full_length * (norm_sq + EPSILON))
    real_s = spectrum[0][None]
    imag_s = spectrum[1][None]
    real_h = masked[0][:, None]
    imag_h = masked[1][:, None]
    filtered = jnp.stack((real_s * real_h + imag_s * imag_h, imag_s * real_h - real_s * imag_h))
    filtered = filtered * scaling[None, :, None, None, None]
    back_pass = dft_last(filtered, 1.0, INNER)
    bin_index = lane_index * local_side + jnp.arange(local_side, dtype=jnp.int32)
    cos_back, sin_back = phase_table(bin_index, every_side, full_length, 1.0)
    back_pass = rotate(back_pass, cos_back, sin_back)
    column_rows = lax.all_to_all(back_pass, "tm", split_axis=4, concat_axis=3, tiled=True)
    series = dft_last(jnp.swapaxes(column_rows, 3, 4), 1.0, INNER)
    timed = lax.all_to_all(series, "tm", split_axis=4, concat_axis=3, tiled=True)
    power = jnp.sum(timed[0] * timed[0] + timed[1] * timed[1], axis=1)
    snr_power = jnp.swapaxes(power, 1, 2).reshape(power.shape[0], local_side * side_length)
    bank_peak = lax.pmax(jnp.max(snr_power, axis=0), "tmpl")
    return (snr_power, bank_peak)


def solution(mesh):
    in_specs = (P(None, None, "tm"), P(None, "tmpl", "tm", None), P("tmpl", None), P("tmpl"))
    out_specs = (P("tmpl", "tm"), P("tm"))
    return jax.shard_map(local, mesh=mesh, in_specs=in_specs, out_specs=out_specs, check_vma=False)
```

profile of v0, /device:TPU:32, one launch (start us, length us, event | category | flops | bytes accessed | tf_op | source)
XLA Modules:
  0.0 850.5 jit_solution(7891186218471136288)
XLA Ops:
  18.1 8.8 %reshape.721 = f32[32,1,24576]{2,1,0:T(1,128)} reshape(f32[2048,3,2,64]{3,2,1,0:T(2,128)} %bitcast.198) | data formatting | bytes 6291456
  26.9 11.9 %all-to-all-start = ((f32[32,1,24576]{2,1,0:T(1,128)}), f32[32,1,24576]{2,1,0:T(1,128)}, u32[]{:S(2)}, u32[]{:S(2)}) async-start(f32[32,1,24576]{2,1,0:T(1,128)} %reshape.721), calls=%async_computation | async-start | bytes 6291456 | tf_op jit(solution)/shard_map/all_to_all | solution.py:59
  41.6 8.7 %multiply_cosine_fusion = (f32[64,2048]{0,1:T(8,128)S(1)}, f32[64,2048]{0,1:T(8,128)}, f32[64,2048]{0,1:T(8,128)}, f32[64,2048]{0,1:T(8,128)}) fusion(s32[64]{0:T(128)S(1)} %iota_add_fusion), kind=kLoop, calls=%fused_computation.63 | loop fusion | flops 1966080 | bytes 2097408 | tf_op jit(solution)/shard_map/cos | solution.py:18
  50.4 60.5 %all-to-all-done = f32[32,1,24576]{2,1,0:T(1,128)} async-done(((f32[32,1,24576]{2,1,0:T(1,128)}), f32[32,1,24576]{2,1,0:T(1,128)}, u32[]{:S(2)}, u32[]{:S(2)}) %all-to-all-start) | async-done | bytes 3145760 | tf_op jit(solution)/shard_map/all_to_all | solution.py:59
  111.4 12.0 %reduce.4 = f32[32,24576]{1,0:T(8,128)} reduce(f32[32,1,24576]{2,1,0:T(1,128)} %all-to-all-done, f32[]{:T(128)} %broadcast.888), dimensions={1}, to_apply=%all_to_all.50.reduce_sub_computation | reduce | bytes 6291460 | tf_op jit(solution)/shard_map/all_to_all | solution.py:59
  131.0 9.1 %copy.275 = f32[2,3,64,32,64]{2,3,4,1,0:T(8,128)} copy(f32[2,3,64,32,64]{2,0,1,4,3:T(2,128)} %bitcast.199) | data formatting | bytes 6291456 | tf_op jit(solution)/shard_map/all_to_all | solution.py:59
  152.6 7.7 copy.181
  200.5 17.4 %copy.280 = f32[2,3,64,2048]{2,0,1,3:T(2,128)} copy(f32[2,3,64,2048]{2,1,3,0:T(4,128)S(1)} %pad_maximum_fusion) | data formatting | bytes 6291456 | tf_op jit(solution)/shard_map/stack | solution.py:24
  217.9 8.8 %reshape.723 = f32[32,1,24576]{2,1,0:T(1,128)} reshape(f32[2048,3,2,64]{3,2,1,0:T(2,128)} %bitcast.201) | data formatting | bytes 6291456
  239.4 118.4 %psum.7 = f32[1]{0:T(128)} all-reduce(f32[1]{0:T(128)} %bitcast.47), channel_id=1, replica_groups=mesh['tm'=32,'tmpl'=8] {'tm'}, use_global_device_ids=true, to_apply=%region_1.2 | all-reduce | flops 1 | bytes 8 | tf_op jit(solution)/shard_map/psum | solution.py:73
  383.2 12.0 %reduce.5 = f32[32,24576]{1,0:T(8,128)} reduce(f32[32,1,24576]{2,1,0:T(1,128)} %all-to-all-done.1, f32[]{:T(128)} %broadcast.888), dimensions={1}, to_apply=%all_to_all.54.reduce_sub_computation | reduce | bytes 6291460 | tf_op jit(solution)/shard_map/all_to_all | solution.py:64
  402.9 9.1 %copy.277 = f32[2,3,64,32,64]{2,3,4,1,0:T(8,128)} copy(f32[2,3,64,32,64]{2,0,1,4,3:T(2,128)} %bitcast.202) | data formatting | bytes 6291456 | tf_op jit(solution)/shard_map/all_to_all | solution.py:64
  424.5 7.7 copy.187
  489.0 17.4 %copy.279 = f32[2,1,3,64,2048]{3,0,2,1,4:T(2,128)} copy(f32[2,1,3,64,2048]{3,2,4,1,0:T(4,128)S(1)} %pad_maximum_fusion.1) | data formatting | bytes 6291456 | tf_op jit(solution)/shard_map/stack | solution.py:24
  506.3 8.8 %reshape.725 = f32[32,1,24576]{2,1,0:T(1,128)} reshape(f32[2048,1,3,2,64]{4,3,2,1,0:T(2,128)} %bitcast.204) | data formatting | bytes 6291456
  515.1 73.7 %all_to_all.69 = f32[32,1,24576]{2,1,0:T(1,128)} all-to-all(f32[32,1,24576]{2,1,0:T(1,128)} %reshape.725), channel_id=1, replica_groups=mesh['tm'=32,'tmpl'=8] {'tm'}, dimensions={0} | all-to-all | bytes 6291456 | tf_op jit(solution)/shard_map/all_to_all | solution.py:85
  588.8 12.0 %reduce.6 = f32[32,24576]{1,0:T(8,128)} reduce(f32[32,1,24576]{2,1,0:T(1,128)} %all_to_all.69, f32[]{:T(128)} %broadcast.888), dimensions={1}, to_apply=%all_to_all.58.reduce_sub_computation | reduce | bytes 6291460 | tf_op jit(solution)/shard_map/all_to_all | solution.py:85
  608.4 9.1 %copy.276 = f32[2,1,3,64,32,64]{3,4,5,2,0,1:T(8,128)} copy(f32[2,1,3,64,32,64]{3,0,2,5,4,1:T(2,128)} %bitcast.205) | data formatting | bytes 6291456 | tf_op jit(solution)/shard_map/all_to_all | solution.py:85
  655.1 9.5 %reshape.700 = f32[2,1,3,64,2048]{3,2,4,0,1:T(4,128)} reshape(f32[2,192,64,32]{1,3,2,0:T(8,128)} %copy.208) | data formatting | bytes 6291456 | tf_op jit(solution)/shard_map/reshape | solution.py:48
  664.6 11.4 %copy.278 = f32[2,1,3,64,2048]{3,0,2,1,4:T(2,128)} copy(f32[2,1,3,64,2048]{3,2,4,0,1:T(4,128)} %reshape.700) | data formatting | bytes 6291456 | tf_op jit(solution)/shard_map/reshape | solution.py:48
  676.0 9.1 %reshape.727 = f32[32,1,24576]{2,1,0:T(1,128)} reshape(f32[2048,1,3,2,64]{4,3,2,1,0:T(2,128)} %bitcast.207) | data formatting | bytes 6291456
  685.1 63.4 %all_to_all.70 = f32[32,1,24576]{2,1,0:T(1,128)S(1)} all-to-all(f32[32,1,24576]{2,1,0:T(1,128)} %reshape.727), channel_id=1, replica_groups=mesh['tm'=32,'tmpl'=8] {'tm'}, dimensions={0} | all-to-all | bytes 6291456 | tf_op jit(solution)/shard_map/all_to_all | solution.py:87
  748.5 10.9 %reduce.7 = f32[32,24576]{1,0:T(8,128)} reduce(f32[32,1,24576]{2,1,0:T(1,128)S(1)} %all_to_all.70, f32[]{:T(128)} %broadcast.888), dimensions={1}, to_apply=%all_to_all.62.reduce_sub_computation | reduce | bytes 6291460 | tf_op jit(solution)/shard_map/all_to_all | solution.py:87
  779.1 62.4 %all-reduce.2.cloned.1.call-done = f32[131072]{0:T(1024)} async-done(((f32[131072]{0:T(1024)}), f32[131072]{0:T(1024)}) %all-reduce.2.cloned.1.call-update) | async-done | bytes 524304 | tf_op jit(solution)/shard_map/pmax | solution.py:90
  (94 shorter events, 254.9 us)
Async XLA Ops:
  26.9 83.9 %all-to-all-start = ((f32[32,1,24576]{2,1,0:T(1,128)}), f32[32,1,24576]{2,1,0:T(1,128)}, u32[]{:S(2)}, u32[]{:S(2)}) async-start(f32[32,1,24576]{2,1,0:T(1,128)} %reshape.721), calls=%async_computation | async-start | bytes 6291456 | tf_op jit(solution)/shard_map/all_to_all | solution.py:59
  160.3 5.8 copy-start
  226.7 7.4 copy-start.7
  226.7 156.6 %all-to-all-start.1 = ((f32[32,1,24576]{2,1,0:T(1,128)}), f32[32,1,24576]{2,1,0:T(1,128)}, u32[]{:S(2)}, u32[]{:S(2)}) async-start(f32[32,1,24576]{2,1,0:T(1,128)} %reshape.723), calls=%async_computation.1 | async-start | bytes 6291456 | tf_op jit(solution)/shard_map/all_to_all | solution.py:64
  233.3 608.2 %all-reduce.2.cloned.1.call-start = ((), (), s32[]{:S(2)}) async-start(), calls=%async_computation.4 | async-start | bytes 1048576 | tf_op jit(solution)/shard_map/pmax | solution.py:90
  432.2 6.0 copy-start.1
  445.9 2.5 copy-start.5
  445.9 2.5 copy-start.6
  451.1 3.9 copy-start.2
  451.1 3.9 copy-start.3
  637.7 5.8 copy-start.4
Sparse Core Ops, SparseCore 0:
  777.9 63.5 all-reduce.1
where the time goes:
time: 858 us; the launch traced here: 850 us
  local copies, waits for them, and re-layouts  302 us (35%)
  blocking collectives  255 us (30%)
  waiting for transfers between devices  123 us (14%)
  other arithmetic  85.9 us (10%)
  matrix products  50 us (6%)
  starting transfers between devices  18.6 us (2%)
  between operations  16 us (2%)
    psum x1, blocking collectives, local(): norm_sq = lax.psum(local_norm, 'tm')  118 us
    all_to_all x1, blocking collectives, local(): lax.all_to_all(back_pass, 'tm', split_axis=4, concat_axis=3, tiled=True)  73.7 us
    unnamed x27, local copies, waits for them, and re-layouts  70.2 us
    all_to_all x1, blocking collectives, local(): lax.all_to_all(series, 'tm', split_axis=4, concat_axis=3, tiled=True)  63.4 us
    pmax x1, waiting for transfers between devices, local(): bank_peak = lax.pmax(jnp.max(snr_power, axis=0), 'tmpl')  62.4 us
    all_to_all x1, waiting for transfers between devices, local(): lax.all_to_all(segment, 'tm', split_axis=3, concat_axis=2, tiled=True)  60.5 us
    reshape x6, local copies, waits for them, and re-layouts, dft_last(): folded = stacked.reshape(2, middle, first_factor, second_factor)  41.5 us
    another operation x2, local copies, waits for them, and re-layouts, rotate(): return jnp.stack((real_part, imag_part))  34.8 us
  transfers between devices with their start and end apart: 3, of which 2 were waited for; matrix products, arithmetic and copies ran while one was open for 5% of the time, Pallas kernels for 0%

commit v1 on v0

v1 whole, which is shorter than its diff:
```python
import functools
import math

import jax
import jax.numpy as jnp
import numpy as np
from jax import lax
from jax.experimental import pallas as pl
from jax.experimental.pallas import tpu as pltpu
from jax.sharding import PartitionSpec as P

EPSILON = 1e-06
SIDE = 2048
FULL = SIDE * SIDE
RANKS = 32
GROUPS = 8
F32 = jnp.float32
BF16 = jnp.bfloat16
VMEM_LIMIT = 56 * 1024 * 1024


def split_table(table):
    high = table.astype(np.float32).astype(jnp.bfloat16)
    low = (table - high.astype(np.float64)).astype(np.float32).astype(jnp.bfloat16)
    return np.stack((high, low))


def section_table(orient, copies):
    sample = np.arange(64)
    order = np.array([2 * (m % 32) + m // 32 for m in range(64)])
    theta = 2.0 * np.pi * np.outer(sample, order) / 64.0
    cosine, sine = np.cos(theta), orient * np.sin(theta)
    eye = np.eye(copies)
    whole = np.block([[np.kron(eye, cosine), np.kron(eye, sine)], [np.kron(eye, -sine), np.kron(eye, cosine)]])
    return split_table(whole)


def column_table():
    dl = np.arange(16)[:, None, None]
    dh = np.arange(128)[None, :, None]
    b = np.arange(128)[None, None, :]
    theta = 2.0 * np.pi * ((b * (dl + 16 * dh)) % SIDE) / SIDE
    cosine, sine = np.cos(theta), np.sin(theta)
    whole = np.concatenate(
        (np.concatenate((cosine, sine), axis=2), np.concatenate((-sine, cosine), axis=2)), axis=1
    )
    return np.swapaxes(split_table(whole), 0, 1)


def row_twiddle():
    theta = 2.0 * np.pi * np.outer(np.arange(32), np.arange(128) % 64) / SIDE
    return np.stack((np.cos(theta), np.sin(theta))).astype(np.float32)


def phases(first, second, orient):
    angle = (first * second % FULL).astype(F32) * (orient * 2.0 * math.pi / FULL)
    return jnp.stack((jnp.cos(angle), jnp.sin(angle)))


def times_unit(value, numer, denom, orient):
    re, im = value
    numer = numer % denom
    if numer == 0:
        return value
    if 8 * numer % denom == 0:
        eighth = 8 * numer // denom
        if eighth == 4:
            return -re, -im
        if eighth in (2, 6):
            return (-im, re) if (eighth == 2) == (orient > 0) else (im, -re)
    cosine = math.cos(2.0 * math.pi * numer / denom)
    sine = orient * math.sin(2.0 * math.pi * numer / denom)
    return re * cosine - im * sine, re * sine + im * cosine


def butterfly(values, orient):
    count = len(values)
    if count == 1:
        return values
    if count == 2:
        (ar, ai), (br, bi) = values
        return [(ar + br, ai + bi), (ar - br, ai - bi)]
    if count == 4:
        (ar, ai), (br, bi), (cr, ci), (dr, di) = values
        sr, si, tr, ti = ar + cr, ai + ci, ar - cr, ai - ci
        ur, ui, vr, vi = br + dr, bi + di, br - dr, bi - di
        if orient > 0:
            return [(sr + ur, si + ui), (tr - vi, ti + vr), (sr - ur, si - ui), (tr + vi, ti - vr)]
        return [(sr + ur, si + ui), (tr + vi, ti - vr), (sr - ur, si - ui), (tr - vi, ti + vr)]
    radix = 4 if count % 4 == 0 else 2
    inner = count // radix
    parts = [butterfly(values[s::radix], orient) for s in range(radix)]
    out = [None] * count
    for k in range(inner):
        joined = butterfly([times_unit(parts[s][k], s * k, count, orient) for s in range(radix)], orient)
        for part in range(radix):
            out[k + inner * part] = joined[part]
    return out


def halves(value):
    high = value.astype(BF16)
    return high, (value - high.astype(F32)).astype(BF16)


def dot(a, b, contract=((1,), (0,))):
    return lax.dot_general(a, b, (contract, ((), ())), preferred_element_type=F32)


def low_lanes(shape):
    return lax.broadcasted_iota(jnp.int32, shape, 1) < 64


def swap(value):
    return pltpu.roll(value, 64, 1)


def tile_rows(start):
    return pl.ds(pl.multiple_of(start, 8), 8)


def gather_columns(group_ref, strain_ref, out_ref):
    first = group_ref[0] * 4

    def piece(detector, tile, part):
        return strain_ref[pl.ds(detector * 2048 + first + tile * 2 + part, 64, stride=32), :]

    for tile in range(2):
        for at, (one, two) in enumerate((((0, 0), (1, 0)), ((0, 1), (1, 1)), ((2, 0), (2, 1)))):
            joined = jnp.concatenate((piece(one[0], tile, one[1]), piece(two[0], tile, two[1])), axis=0)
            out_ref[16 * tile:16 * tile + 16, 8 * at:8 * at + 8, :] = joined.T.reshape(16, 8, 128)


def prepare_templates(weight_ref, template_ref, out_ref, norm_ref):
    total = jnp.zeros((64, 128), F32)
    for chunk in range(16):
        lanes = slice(128 * chunk, 128 * chunk + 128)
        weight = weight_ref[:, lanes]
        for part in range(2):
            value = template_ref[part, :, lanes] * weight
            total = total + value * value
            out_ref[part, lanes, :] = jnp.concatenate((value, value), axis=0).T
    norm_ref[...] = jnp.sum(total.reshape(8, 8, 128), axis=0)


def first_section(in_ref, twiddle_ref, wide_ref, narrow_ref, phase_ref, out_ref, pair_ref, single_ref, turn_ref):
    lower = low_lanes((8, 128))
    for at in range(2):
        values = []
        for rank in range(RANKS):
            if at == 0:
                values.append((in_ref[rank, 0:8, :], in_ref[rank, 8:16, :]))
            else:
                one = in_ref[rank, 16:24, :]
                values.append((one, swap(one)))
        for digit, (re, im) in enumerate(butterfly(values, -1)):
            cosine, sine = twiddle_ref[0, digit:digit + 1, :], twiddle_ref[1, digit:digit + 1, :]
            re, im = re * cosine + im * sine, im * cosine - re * sine
            rows = slice(8 * digit, 8 * digit + 8)
            if at == 0:
                pair_ref[rows, 0:128] = re
                pair_ref[rows, 128:256] = im
            else:
                single_ref[rows, :] = jnp.where(lower, re, swap(im))
    high, low = halves(pair_ref[...])
    pair = dot(high, wide_ref[0]) + dot(low, wide_ref[0]) + dot(high, wide_ref[1])
    high, low = halves(single_ref[...])
    single = dot(high, narrow_ref[0]) + dot(low, narrow_ref[0]) + dot(high, narrow_ref[1])
    cosine, sine = phase_ref[0], phase_ref[1]
    re, im = pair[:, 0:128], pair[:, 128:256]
    turn_ref[0] = re * cosine - im * sine
    turn_ref[1] = im * cosine + re * sine
    turn_ref[2] = single * cosine + swap(single) * jnp.where(low_lanes((256, 128)), -sine, sine)
    for at in range(3):
        for quad in range(2):
            cols = [turn_ref[at, pl.ds(4 * quad + u, 32, stride=8), :] for u in range(4)]
            stacked = jnp.concatenate(
                [jnp.concatenate([c[:, 32 * s:32 * s + 32] for c in cols], axis=1) for s in range(4)], axis=0
            )
            turned = stacked.T
            for u in range(4):
                out_ref[pl.ds(8 * at + 4 * quad + u, 32, stride=24), :] = turned[32 * u:32 * u + 32, :]


def middle_section(in_ref, template_ref, near_ref, far_ref, table_hbm, out_ref, work_ref, table_ref, table_sem):
    copy = pltpu.make_async_copy(table_hbm, table_ref, table_sem)
    copy.start()

    def spread(low, carry):
        for at in range(2):
            values = []
            for a in range(16):
                rank = 16 * (a % 2) + low
                if at == 0:
                    values.append((in_ref[a // 2, rank, 0:8, :], in_ref[a // 2, rank, 8:16, :]))
                else:
                    one = in_ref[a // 2, rank, 16:24, :]
                    values.append((one, swap(one)))
            for digit, (re, im) in enumerate(butterfly(values, -1)):
                work_ref[digit, tile_rows(8 * low), 128 * at:128 * at + 128] = re
                work_ref[digit, tile_rows(128 + 8 * low), 128 * at:128 * at + 128] = im
        return carry

    lax.fori_loop(0, 16, spread, 0)
    copy.wait()

    def filter_digit(digit, carry):
        table_high, table_low = table_ref[digit, 0], table_ref[digit, 1]
        high, low = halves(work_ref[digit])
        spectrum = dot(table_high, high) + dot(table_high, low) + dot(table_low, high)
        h_re = template_ref[0, pl.ds(digit, 128, stride=16), :]
        h_im = template_ref[1, pl.ds(digit, 128, stride=16), :]
        h_re = jnp.concatenate((h_re, h_re), axis=1)
        h_im = jnp.concatenate((h_im, h_im), axis=1)
        s_re, s_im = spectrum[0:128], spectrum[128:256]
        product = jnp.concatenate((s_re * h_re + s_im * h_im, s_im * h_re - s_re * h_im), axis=0)
        high, low = halves(product)
        turn = ((0,), (0,))
        series = dot(table_high, high, turn) + dot(table_high, low, turn) + dot(table_low, high, turn)
        cosine = jnp.concatenate((near_ref[0], near_ref[0]), axis=1)
        sine = jnp.concatenate((near_ref[1], near_ref[1]), axis=1)
        re, im = series[0:128], series[128:256]
        work_ref[digit, 0:128, :] = re * cosine - im * sine
        work_ref[digit, 128:256, :] = re * sine + im * cosine
        return carry

    lax.fori_loop(0, 16, filter_digit, 0)
    lower = low_lanes((8, 128))

    def finish(values, row, part_rows, base, half):
        for digit, (re, im) in enumerate(butterfly(values, 1)):
            cosine, sine = far_ref[0, digit:digit + 1, :], far_ref[1, digit:digit + 1, :]
            out_ref[2 * digit + half, tile_rows(base + row), :] = re * cosine - im * sine
            out_ref[2 * digit + half, tile_rows(base + part_rows + row), :] = re * sine + im * cosine

    def collect_pair(step, carry):
        for half in range(2):
            rows = 64 * half + 8 * step
            values = [
                (work_ref[d, tile_rows(rows), 0:128], work_ref[d, tile_rows(128 + rows), 0:128]) for d in range(16)
            ]
            finish(values, 8 * step, 64, 0, half)
        return carry

    lax.fori_loop(0, 8, collect_pair, 0)

    def collect_single(step, carry):
        for half in range(2):
            rows = 64 * half + 8 * step
            values = []
            for d in range(16):
                both = []
                for part in range(2):
                    one = work_ref[d, tile_rows(128 * part + rows), 128:256]
                    two = work_ref[d, tile_rows(128 * part + rows + 32), 128:256]
                    both.append(jnp.where(lower, one, swap(two)))
                values.append(tuple(both))
            finish(values, 8 * step, 32, 128, half)
        return carry

    lax.fori_loop(0, 4, collect_single, 0)


def last_section(in_ref, twiddle_ref, wide_ref, norm_ref, out_ref, pair_ref, single_ref):
    def spread(work_ref, base, part_rows):
        def step_fn(step, carry):
            values = [
                (in_ref[r, tile_rows(base + 8 * step), :], in_ref[r, tile_rows(base + part_rows + 8 * step), :])
                for r in range(RANKS)
            ]
            for digit, (re, im) in enumerate(butterfly(values, 1)):
                cosine, sine = twiddle_ref[0, digit:digit + 1, :], twiddle_ref[1, digit:digit + 1, :]
                rows = tile_rows(part_rows * digit + 8 * step)
                work_ref[rows, 0:128] = re * cosine - im * sine
                work_ref[rows, 128:256] = im * cosine + re * sine
            return carry

        lax.fori_loop(0, part_rows // 8, step_fn, 0)

    spread(pair_ref, 0, 64)
    spread(single_ref, 128, 32)

    def power_of(value):
        high, low = halves(value)
        full = dot(high, wide_ref[0]) + dot(low, wide_ref[0]) + dot(high, wide_ref[1])
        re, im = full[:, 0:128], full[:, 128:256]
        return re * re + im * im

    lower = low_lanes((32, 128))

    def combine(quad, carry):
        pair = power_of(pair_ref[pl.ds(pl.multiple_of(256 * quad, 256), 256), :])
        single = power_of(single_ref[pl.ds(pl.multiple_of(128 * quad, 128), 128), :]).T
        for two in range(2):
            turned = pair[128 * two:128 * two + 128].T
            summed = turned[0:64] + turned[64:128]
            even, odd = summed[0:32], summed[32:64]
            both = (jnp.where(lower, even, swap(odd)), jnp.where(lower, swap(even), odd))
            for one in range(2):
                u = 2 * two + one
                lanes = slice(32 * u, 32 * u + 32)
                rest = jnp.concatenate(
                    (single[0:32, lanes], single[64:96, lanes], single[32:64, lanes], single[96:128, lanes]), axis=1
                )
                out_ref[pl.ds(4 * quad + u, 32, stride=40), :] = both[one] + rest
        return carry

    lax.fori_loop(0, 8, combine, 0)
    norm = norm_ref[...]
    for rank in range(RANKS):
        out_ref[40 * rank + 32:40 * rank + 40, :] = norm


def place_samples(in_ref, out_ref):
    total = jnp.zeros((8, 128), F32)
    for rank in range(RANKS):
        total = total + in_ref[rank, 32:40, :]
    scale = 1.0 / (FULL * (jnp.sum(total) + EPSILON))
    lower = low_lanes((32, 128))
    for two in range(16):
        one = in_ref[2 * two, 0:32, :] * scale
        other = in_ref[2 * two + 1, 0:32, :] * scale
        out_ref[pl.ds(two, 32, stride=16), :] = jnp.where(lower, one, swap(other))
        out_ref[pl.ds(512 + two, 32, stride=16), :] = jnp.where(lower, swap(one), other)


PARAMS = pltpu.CompilerParams(vmem_limit_bytes=VMEM_LIMIT)


def shape(*dims):
    return jax.ShapeDtypeStruct(dims, F32)


def call(kernel, out, specs, scratch=(), **kwargs):
    many = isinstance(out, (tuple, list))
    whole = pl.BlockSpec(memory_space=pltpu.VMEM)
    return pl.pallas_call(
        kernel,
        out_shape=out,
        in_specs=specs,
        out_specs=[whole] * len(out) if many else whole,
        scratch_shapes=list(scratch),
        compiler_params=PARAMS,
        **kwargs,
    )


def cost(us):
    return pl.CostEstimate(flops=int(us * 1e9), bytes_accessed=int(us * 1e6), transcendentals=0)


def group_peak(values):
    rows = values.shape[0]
    me = lax.axis_index("tmpl")
    core, y = me % 2, me // 2
    half, part = rows // 2, rows // 8
    across = [(i, i ^ 1) for i in range(GROUPS)]

    def around(step):
        return [(i, ((i // 2 + step) % 4) * 2 + i % 2) for i in range(GROUPS)]

    mine = lax.dynamic_slice_in_dim(values, core * half, half, 0)
    other = lax.dynamic_slice_in_dim(values, (1 - core) * half, half, 0)
    mine = jnp.maximum(mine, lax.ppermute(other, "tmpl", across))
    parts = mine.reshape(4, part, 128)
    got = [
        lax.ppermute(lax.dynamic_index_in_dim(parts, (y + s) % 4, 0, False), "tmpl", around(s)) for s in (1, 2, 3)
    ]
    best = lax.dynamic_index_in_dim(parts, y, 0, False)
    for one in got:
        best = jnp.maximum(best, one)
    spread = [best] + [lax.ppermute(best, "tmpl", around(s)) for s in (1, 2, 3)]
    full = jnp.zeros((4, part, 128), values.dtype)
    for step, one in enumerate(spread):
        full = lax.dynamic_update_index_in_dim(full, one, (y - step) % 4, 0)
    far = lax.ppermute(full, "tmpl", across)
    first = jnp.where(core == 0, full, far)
    second = jnp.where(core == 0, far, full)
    return jnp.concatenate((first, second), axis=0).reshape(rows, 128)


def local(strain, templates, pattern, cutoff):
    me = lax.axis_index("tm")
    group = lax.axis_index("tmpl")
    vmem = pl.BlockSpec(memory_space=pltpu.VMEM)
    smem = pl.BlockSpec(memory_space=pltpu.SMEM)
    anywhere = pl.BlockSpec(memory_space=pl.ANY)

    samples = strain.reshape(2, 3, 64, 16, 128).transpose(1, 2, 3, 0, 4).reshape(6144, 128)
    columns = call(gather_columns, shape(RANKS, 24, 128), [smem, vmem], cost_estimate=cost(3))(
        group.astype(jnp.int32).reshape(1), samples
    )
    columns = lax.all_to_all(columns, "tm", 0, 0, tiled=True)

    block_index = jnp.arange(pattern.shape[1], dtype=jnp.int32)
    active = pattern.astype(F32) * (block_index[None, :] < cutoff[:, None]).astype(F32)
    weight = jnp.repeat(active, SIDE // pattern.shape[1], axis=1)
    bank, norm = call(
        prepare_templates, (shape(2, SIDE, 128), shape(8, 128)), [vmem, vmem], cost_estimate=cost(4)
    )(weight, templates.reshape(2, 64, SIDE))

    row = jnp.arange(256, dtype=jnp.int32)[:, None]
    lane = jnp.arange(128, dtype=jnp.int32)[None, :]
    bin_at = row // 8 + 32 * (2 * (lane % 32) + lane // 32 % 2)
    first_phase = phases(256 * group + 8 * me + row % 8, bin_at, -1.0)
    bin_mine = 64 * me + lane % 64
    near = phases(jnp.arange(128, dtype=jnp.int32)[:, None], bin_mine, 1.0)
    far = phases(128 * jnp.arange(16, dtype=jnp.int32)[:, None], bin_mine, 1.0)
    twiddle = jnp.asarray(row_twiddle())

    rows = call(
        first_section,
        shape(RANKS * 24, 128),
        [vmem] * 5,
        [pltpu.VMEM((256, 256), F32), pltpu.VMEM((256, 128), F32), pltpu.VMEM((3, 256, 128), F32)],
        cost_estimate=cost(4),
    )(columns, twiddle, jnp.asarray(section_table(-1.0, 2)), jnp.asarray(section_table(-1.0, 1)), first_phase)
    rows = lax.all_to_all(rows.reshape(RANKS, 24, 128), "tm", 0, 0, tiled=True)
    rows = lax.all_gather(rows, "tmpl", axis=0)

    series = call(
        middle_section,
        shape(RANKS, 192, 128),
        [vmem] * 4 + [anywhere],
        [
            pltpu.VMEM((16, 256, 256), F32),
            pltpu.VMEM((16, 2, 256, 256), BF16),
            pltpu.SemaphoreType.DMA,
        ],
        cost_estimate=cost(10),
    )(rows, bank, near, far, jnp.asarray(column_table()))
    series = lax.all_to_all(series, "tm", 0, 0, tiled=True)

    power = call(
        last_section,
        shape(RANKS * 40, 128),
        [vmem] * 4,
        [pltpu.VMEM((2048, 256), F32), pltpu.VMEM((1024, 256), F32)],
        cost_estimate=cost(8),
    )(series, twiddle, jnp.asarray(section_table(1.0, 2)), norm)
    power = lax.all_to_all(power.reshape(RANKS, 40, 128), "tm", 0, 0, tiled=True)
    snr = call(place_samples, shape(1024, 128), [vmem], cost_estimate=cost(2))(power)
    peak = group_peak(snr)
    return snr.reshape(1, 64 * SIDE), peak.reshape(64 * SIDE)


def solution(mesh):
    in_specs = (P(None, None, "tm"), P(None, "tmpl", "tm", None), P("tmpl", None), P("tmpl"))
    out_specs = (P("tmpl", "tm"), P("tm"))
    return jax.shard_map(local, mesh=mesh, in_specs=in_specs, out_specs=out_specs, check_vma=False)
```

time: 858 us -> 256 us (0.30)
  local copies, waits for them, and re-layouts: 302 us -> 3.74 us
  blocking collectives: 255 us -> 102 us
  other arithmetic: 85.9 us -> 4.91 us
  waiting for transfers between devices: 123 us -> 63.7 us
  matrix products: 50 us -> 0 us
  Pallas kernels: 0 us -> 39.4 us
    psum x1 -> x0, blocking collectives: 118 us -> none  [local(): norm_sq = lax.psum(local_norm, 'tm')]
    reshape x10 -> x0, local copies, waits for them, and re-layouts: 73.3 us -> none  [the longest x6 41.5 us: dft_last(): folded = stacked.reshape(2, middle, first_factor, second_factor)]
    unnamed x27 -> x6, local copies, waits for them, and re-layouts: 70.2 us -> 1.6 us
    pmax x1 -> x0, waiting for transfers between devices: 62.4 us -> none  [local(): bank_peak = lax.pmax(jnp.max(snr_power, axis=0), 'tmpl')]
    all_to_all x8 -> x0, local copies, waits for them, and re-layouts: 52.1 us -> none  [the longest x3 16 us: local(): lax.all_to_all(segment, 'tm', split_axis=3, concat_axis=2, tiled=True)]
    dot_general x8 -> x0, matrix products: 50 us -> none  [the longest x4 28.5 us: dft_last(): jnp.einsum('qmkb,qrkbj->rmjk', section_one, table_two, precision=HIGHEST)]
    all_to_all x4 -> x0, other arithmetic: 46.7 us -> none  [the longest x1 12 us: local(): lax.all_to_all(first_pass, 'tm', split_axis=3, concat_axis=2, tiled=True)]
    pallas_call x0 -> x6, Pallas kernels: none -> 39.4 us  [the longest x1 19.3 us: local(): call(middle_section, shape(RANKS, 192, 128), [vmem] * 4 + [anywhere], [pl...]
  transfers between devices with their start and end apart: 3 -> 11, of which waited for: 2 -> 10; matrix products, arithmetic and copies ran while one was open for 5% -> 2% of each run, Pallas kernels for 0% -> 1%
where the time goes in v1:
time: 256 us; the launch traced here: 253 us
  blocking collectives  102 us (40%)
  waiting for transfers between devices  63.7 us (25%)
  Pallas kernels  39.4 us (15%)
  starting transfers between devices  24.8 us (10%)
  between operations  15 us (6%)
  other arithmetic  4.91 us (2%)
  local copies, waits for them, and re-layouts  3.74 us (1%)
    all_to_all x1, blocking collectives, local(): series = lax.all_to_all(series, 'tm', 0, 0, tiled=True)  82.7 us
    all_gather x1, waiting for transfers between devices, local(): rows = lax.all_gather(rows, 'tmpl', axis=0)  20.1 us
    pallas_call x1, Pallas kernels, local(): call(middle_section, shape(RANKS, 192, 128), [vmem] * 4 + [anywhere], [pl...  19.3 us
    all_to_all x1, blocking collectives, local(): rows = lax.all_to_all(rows.reshape(RANKS, 24, 128), 'tm', 0, 0, tiled=True)  18.9 us
    all_to_all x1, waiting for transfers between devices, local(): lax.all_to_all(power.reshape(RANKS, 40, 128), 'tm', 0, 0, tiled=True)  18.8 us
    all_to_all x1, waiting for transfers between devices, local(): columns = lax.all_to_all(columns, 'tm', 0, 0, tiled=True)  13.3 us
    all_to_all x1, starting transfers between devices, local(): columns = lax.all_to_all(columns, 'tm', 0, 0, tiled=True)  11.2 us
    pallas_call x1, Pallas kernels, local(): call(last_section, shape(RANKS * 40, 128), [vmem] * 4, [pltpu.VMEM((2048,...  8.67 us
  transfers between devices with their start and end apart: 11, of which 10 were waited for; matrix products, arithmetic and copies ran while one was open for 2% of the time, Pallas kernels for 1%

profile of v1, /device:TPU:32, one launch (start us, length us, event | category | flops | bytes accessed | tf_op | source)
XLA Modules:
  0.0 253.2 jit_solution(15921265313498068267)
XLA Ops:
  7.2 2.9 %shard_map.104 = f32[32,24,128]{2,1,0:T(8,128)} custom-call(s32[1]{0:T(128)} %bitcast.group_ref, f32[6144,128]{1,0:T(8,128)} %bitcast.44), custom_call_target="tpu_custom_call" | custom-call | flops 3000000000 | bytes 3000000 | tf_op jit(solution)/shard_map/pallas_call | solution.py:390
  10.1 11.2 %all-to-all-start = ((f32[32,24,128]{2,1,0:T(8,128)}), f32[32,24,128]{2,1,0:T(8,128)S(1)}, u32[]{:S(2)}, u32[]{:S(2)}) async-start(f32[32,24,128]{2,1,0:T(8,128)} %shard_map.104), calls=%async_computation | async-start | bytes 786432 | tf_op jit(solution)/shard_map/all_to_all | solution.py:393
  22.8 13.3 %all-to-all-done.in_ref = f32[32,24,128]{2,1,0:T(8,128)S(1)} async-done(((f32[32,24,128]{2,1,0:T(8,128)}), f32[32,24,128]{2,1,0:T(8,128)S(1)}, u32[]{:S(2)}, u32[]{:S(2)}) %all-to-all-start) | async-done | bytes 393248 | tf_op jit(solution)/shard_map/all_to_all | solution.py:393
  36.8 3.0 %shard_map.105 = f32[768,128]{1,0:T(8,128)} custom-call(f32[32,24,128]{2,1,0:T(8,128)} %copy-done.1, f32[2,32,128]{2,1,0:T(8,128)} %constant.225.clone.twiddle_ref, bf16[2,256,256]{2,1,0:T(8,128)(2,1)} %constant.226.clone.wide_ref, bf16[2,128,128]{2,1,0:T(8,128)(2,1)} %constant.227.clone.narrow_ref, f32[2,256,128]{2,1,0:T(8,128)} %pad_maximum_fusion.1.phase_ref), custom_call_target="tpu_custom_call" | custom-call | flops 4000000000 | bytes 4000000 | tf_op jit(solution)/shard_map/pallas_call | solution.py:411
  39.8 18.9 %all_to_all.20 = f32[32,24,128]{2,1,0:T(8,128)} all-to-all(f32[32,24,128]{2,1,0:T(8,128)} %bitcast.42), channel_id=1, replica_groups=mesh['tm'=32,'tmpl'=8] {'tm'}, dimensions={0} | all-to-all | bytes 786432 | tf_op jit(solution)/shard_map/all_to_all | solution.py:418
  59.6 0.9 broadcast_in_dim.28.weight_ref
  62.2 3.2 %shard_map.106 = (f32[2,2048,128]{2,1,0:T(8,128)}, f32[8,128]{1,0:T(8,128)}) custom-call(f32[1,2048]{1,0:T(1,128)} %broadcast_in_dim.28.weight_ref, f32[2,64,2048]{2,1,0:T(8,128)} %bitcast.46), custom_call_target="tpu_custom_call" | custom-call | flops 4000000000 | bytes 4000000 | tf_op jit(solution)/shard_map/pallas_call | solution.py:398
  65.4 20.1 %all-gather.3.cloned.1.call-done = f32[256,24,128]{2,1,0:T(8,128)} async-done(((f32[32,24,128]{2,1,0:T(8,128)}), f32[256,24,128]{2,1,0:T(8,128)}) %all-gather.3.cloned.1.call-update) | async-done | bytes 3145744 | tf_op jit(solution)/shard_map/all_gather | solution.py:419
  85.5 19.3 %shard_map.107 = f32[32,192,128]{2,1,0:T(8,128)} custom-call(f32[8,32,24,128]{3,2,1,0:T(8,128)} %bitcast.45, f32[2,2048,128]{2,1,0:T(8,128)} %get-tuple-element.4.template_ref, f32[2,128,128]{2,1,0:T(8,128)} %pad_maximum_fusion.2.near_ref, f32[2,16,128]{2,1,0:T(8,128)} %pad_maximum_fusion.3.far_ref, bf16[16,2,256,256]{3,2,1,0:T(8,128)(2,1)} %constant.228.clone.table_hbm), custom_call_target="tpu_custom_call" | custom-call | flops 10000000000 | bytes 10000000 | tf_op jit(solution)/shard_map/pallas_call | solution.py:421
  104.8 82.7 %all_to_all.21.in_ref = f32[32,192,128]{2,1,0:T(8,128)} all-to-all(f32[32,192,128]{2,1,0:T(8,128)} %shard_map.107), channel_id=1, replica_groups=mesh['tm'=32,'tmpl'=8] {'tm'}, dimensions={0} | all-to-all | bytes 6291456 | tf_op jit(solution)/shard_map/all_to_all | solution.py:432
  187.5 8.7 %shard_map.108 = f32[1280,128]{1,0:T(8,128)} custom-call(f32[32,192,128]{2,1,0:T(8,128)} %all_to_all.21.in_ref, f32[2,32,128]{2,1,0:T(8,128)} %constant.225.clone.twiddle_ref, bf16[2,256,256]{2,1,0:T(8,128)(2,1)} %constant.229.clone.wide_ref, f32[8,128]{1,0:T(8,128)} %get-tuple-element.5.norm_ref), custom_call_target="tpu_custom_call" | custom-call | flops 8000000000 | bytes 8000000 | tf_op jit(solution)/shard_map/pallas_call | solution.py:434
  196.1 6.5 %all-to-all-start.3 = ((f32[32,40,128]{2,1,0:T(8,128)}), f32[32,40,128]{2,1,0:T(8,128)S(1)}, u32[]{:S(2)}, u32[]{:S(2)}) async-start(f32[32,40,128]{2,1,0:T(8,128)} %bitcast.39), calls=%async_computation.3 | async-start | bytes 1310720 | tf_op jit(solution)/shard_map/all_to_all | solution.py:441
  202.6 18.8 %all-to-all-done.3.in_ref = f32[32,40,128]{2,1,0:T(8,128)S(1)} async-done(((f32[32,40,128]{2,1,0:T(8,128)}), f32[32,40,128]{2,1,0:T(8,128)S(1)}, u32[]{:S(2)}, u32[]{:S(2)}) %all-to-all-start.3) | async-done | bytes 655392 | tf_op jit(solution)/shard_map/all_to_all | solution.py:441
  222.3 2.3 shard_map.109
  224.6 1.0 constant_dynamic-slice_fusion
  225.8 1.4 collective-permute-done
  227.2 1.0 dynamic-slice_maximum_fusion
  228.2 1.7 collective-permute-start.3
  231.5 1.8 collective-permute-done.3
  233.2 2.8 %collective-permute-done.2 = f32[128,128]{1,0:T(8,128)S(1)} collective-permute-done((f32[128,128]{1,0:T(8,128)S(1)}, f32[128,128]{1,0:T(8,128)S(1)}, u32[]{:S(2)}, u32[]{:S(2)}) %collective-permute-start.2) | collective-permute-done | bytes 65568 | tf_op jit(solution)/shard_map/ppermute | solution.py:367
  236.9 2.0 collective-permute-start.5
  238.9 1.6 collective-permute-start.6
  240.4 2.5 collective-permute-done.4
  243.9 1.5 collective-permute-done.7
  (35 shorter events, 9.1 us)
Async XLA Ops:
  10.1 25.9 %all-to-all-start = ((f32[32,24,128]{2,1,0:T(8,128)}), f32[32,24,128]{2,1,0:T(8,128)S(1)}, u32[]{:S(2)}, u32[]{:S(2)}) async-start(f32[32,24,128]{2,1,0:T(8,128)} %shard_map.104), calls=%async_computation | async-start | bytes 786432 | tf_op jit(solution)/shard_map/all_to_all | solution.py:393
  21.3 64.2 %all-gather.3.cloned.1.call-start = ((), (), s32[]{:S(2)}) async-start(), calls=%async_computation.4 | async-start | bytes 3538944 | tf_op jit(solution)/shard_map/all_gather | solution.py:419
  22.7 36.6 %copy-start.2 = (s32[1,1024]{1,0:T(1,128)S(1)}, s32[1,1024]{1,0:T(1,128)}, u32[]{:S(2)}) copy-start(s32[1,1024]{1,0:T(1,128)} %param.11) | copy-start | bytes 12292
  36.0 0.7 copy-start.1
  196.1 25.3 %all-to-all-start.3 = ((f32[32,40,128]{2,1,0:T(8,128)}), f32[32,40,128]{2,1,0:T(8,128)S(1)}, u32[]{:S(2)}, u32[]{:S(2)}) async-start(f32[32,40,128]{2,1,0:T(8,128)} %bitcast.39), calls=%async_computation.3 | async-start | bytes 1310720 | tf_op jit(solution)/shard_map/all_to_all | solution.py:441
  221.4 0.9 copy-start
  225.6 1.6 collective-permute-start
  228.2 5.0 %collective-permute-start.3 = (f32[128,128]{1,0:T(8,128)S(1)}, f32[128,128]{1,0:T(8,128)S(1)}, u32[]{:S(2)}, u32[]{:S(2)}) collective-permute-start(f32[128,128]{1,0:T(8,128)S(1)} %get-tuple-element.11), channel_id=1, source_target_pairs={{0,6},{1,7},{2,0},{3,1},{4,2},{5,3},{6,4},{7,5},{8,14},{9,15},{10,... | collective-permute-start | bytes 196616 | tf_op jit(solution)/shard_map/ppermute | solution.py:367
  229.9 6.2 %collective-permute-start.2 = (f32[128,128]{1,0:T(8,128)S(1)}, f32[128,128]{1,0:T(8,128)S(1)}, u32[]{:S(2)}, u32[]{:S(2)}) collective-permute-start(f32[128,128]{1,0:T(8,128)S(1)} %get-tuple-element.12), channel_id=1, source_target_pairs={{0,4},{1,5},{2,6},{3,7},{4,0},{5,1},{6,2},{7,3},{8,12},{9,13},{10,... | collective-permute-start | bytes 196616 | tf_op jit(solution)/shard_map/ppermute | solution.py:367
  230.8 5.9 %collective-permute-start.1 = (f32[128,128]{1,0:T(8,128)S(1)}, f32[128,128]{1,0:T(8,128)S(1)}, u32[]{:S(2)}, u32[]{:S(2)}) collective-permute-start(f32[128,128]{1,0:T(8,128)S(1)} %get-tuple-element.10), channel_id=1, source_target_pairs={{0,2},{1,3},{2,4},{3,5},{4,6},{5,7},{6,0},{7,1},{8,10},{9,11},{10,... | collective-permute-start | bytes 196616 | tf_op jit(solution)/shard_map/ppermute | solution.py:367
  236.7 6.3 %collective-permute-start.4 = (f32[128,128]{1,0:T(8,128)S(1)}, f32[128,128]{1,0:T(8,128)S(1)}, u32[]{:S(2)}, u32[]{:S(2)}) collective-permute-start(f32[128,128]{1,0:T(8,128)S(1)} %get-tuple-element.7), channel_id=1, source_target_pairs={{0,2},{1,3},{2,4},{3,5},{4,6},{5,7},{6,0},{7,1},{8,10},{9,11},{10,... | collective-permute-start | bytes 196616 | tf_op jit(solution)/shard_map/ppermute | solution.py:372
  236.9 6.1 %collective-permute-start.5 = (f32[128,128]{1,0:T(8,128)S(1)}, f32[128,128]{1,0:T(8,128)S(1)}, u32[]{:S(2)}, u32[]{:S(2)}) collective-permute-start(f32[128,128]{1,0:T(8,128)S(1)} %get-tuple-element.7), channel_id=1, source_target_pairs={{0,4},{1,5},{2,6},{3,7},{4,0},{5,1},{6,2},{7,3},{8,12},{9,13},{10,... | collective-permute-start | bytes 196616 | tf_op jit(solution)/shard_map/ppermute | solution.py:372
  238.9 5.0 %collective-permute-start.6 = (f32[128,128]{1,0:T(8,128)S(1)}, f32[128,128]{1,0:T(8,128)S(1)}, u32[]{:S(2)}, u32[]{:S(2)}) collective-permute-start(f32[128,128]{1,0:T(8,128)S(1)} %get-tuple-element.7), channel_id=1, source_target_pairs={{0,6},{1,7},{2,0},{3,1},{4,2},{5,3},{6,4},{7,5},{8,14},{9,15},{10,... | collective-permute-start | bytes 196616 | tf_op jit(solution)/shard_map/ppermute | solution.py:372
  243.8 1.6 collective-permute-start.7
Sparse Core Ops, SparseCore 0:
  58.8 26.6 all-gather.2
